TPU v7x, 32 devices: a whole 2x2x4 slice. The times are simulated.
32 devices in a mesh: groups: 2 (over y), curve: 16 (over z, x, core).
Axes of the slice: x: 2, y: 2, z: 4, core: 2. Of those that a mesh axis runs over, the one named last changes fastest.
Arguments:
- tracer_mass: float32 [9216, 200], P(('groups', 'curve')), parts along dimension 0, may hold values from 0.1 to 10
- send_ids: int32 [128, 32], P(('groups', 'curve')), parts along dimension 0, may hold values from 0 to 31, as said below
- send_counts: int32 [128], P(('groups', 'curve')), parts along dimension 0, may hold values from 1 to 32, as said below
- sources: int32 [9216, 4], P(('groups', 'curve')), parts along dimension 0, may hold values from 0 to 1439
- fractions: float32 [9216, 4], P(('groups', 'curve')), parts along dimension 0, may hold values from 0.02 to 0.25
- moments: float32 [2, 9216, 4], P(None, ('groups', 'curve')), parts along dimension 1, may hold values from -0.5 to 0.5
Outputs:
- new_mass: float32 [9216, 200], P(('groups', 'curve')), parts along dimension 0
There are 2 independent parts, one for each index of `groups`. A program takes and returns all parts, laid end to end along the dimension named above; each array names one. Nothing has to cross between parts.
Inputs may be any that keep to these rules, and one draw needn't show every extreme that they name: `send_ids`: each row holds distinct local element indices of the owning device. `send_counts`: slots below the count are live; in every draw some lists reach 32. `sources`: indices into the device's own extended cells.
All inputs are finite; a program needn't handle non-finite values.
Results may differ from a plain program's by a relative error of at most 0.0001.
Values sent between devices are 32-bit elements; how exact they have to be, the bound alone decides.
A program may use at most 64 MiB of HBM per device.

v0:
```python
import jax
import jax.numpy as jnp
from jax import lax
from jax.sharding import PartitionSpec as P

OFFSETS = (1, 2, -1, -2)


def from_behind(x, axis, by):
    count = lax.axis_size(axis)
    return lax.ppermute(x, axis, [(i, (i + by) % count) for i in range(count)])


def build_slopes(values):
    count = values.shape[0]
    index = jnp.arange(count, dtype=jnp.int32)
    column = (index % 3)[:, None]
    row_pos = (index // 3 % 3)[:, None]
    right = jnp.roll(values, -1, axis=0)
    left = jnp.roll(values, 1, axis=0)
    below = jnp.roll(values, -3, axis=0)
    above = jnp.roll(values, 3, axis=0)
    slope_x = jnp.where(
        column == 0, right - values, jnp.where(column == 1, 0.5 * (right - left), values - left)
    )
    slope_y = jnp.where(
        row_pos == 0, below - values, jnp.where(row_pos == 1, 0.5 * (below - above), values - above)
    )
    return (slope_x, slope_y)


def transport(extended, sources_dev, fraction_dev, moment_x, moment_y):
    width = extended.shape[-1]
    total_cells = extended.shape[0]
    slope_x, slope_y = build_slopes(extended)
    inflow = jnp.zeros((sources_dev.shape[0], width), jnp.float32)
    outflow = jnp.zeros((total_cells, width), jnp.float32)
    for column in range(sources_dev.shape[1]):
        source = sources_dev[:, column]
        flux = fraction_dev[:, column, None] * (
            extended[source]
            + moment_x[:, column, None] * slope_x[source]
            + moment_y[:, column, None] * slope_y[source]
        )
        inflow = inflow + flux
        outflow = outflow + jax.ops.segment_sum(flux, source, num_segments=total_cells)
    return (inflow, outflow)


def local(tracer_mass, send_ids, send_counts, sources, fractions, moments):
    own_cells = tracer_mass.shape[0]
    width = tracer_mass.shape[1]
    slots = send_ids.shape[1]
    list_cells = 9 * slots
    live = (jnp.arange(slots, dtype=jnp.int32)[None, :] < send_counts[:, None]).astype(jnp.float32)
    cell_ids = (9 * send_ids[:, :, None] + jnp.arange(9, dtype=jnp.int32)[None, None, :]).reshape(
        4, list_cells
    )
    live_cells = (live[:, :, None] * jnp.ones((1, 1, 9), jnp.float32)).reshape(4, list_cells)
    packed = tracer_mass[cell_ids] * live_cells[..., None]
    received = jnp.stack([from_behind(packed[slot], "curve", OFFSETS[slot]) for slot in range(4)])
    extended = jnp.concatenate([tracer_mass, received.reshape(4 * list_cells, width)], axis=0)
    inflow, outflow = transport(extended, sources, fractions, moments[0], moments[1])
    owned = outflow[:own_cells]
    returned = outflow[own_cells:].reshape(4, list_cells, width)
    back = jnp.stack([from_behind(returned[slot], "curve", -OFFSETS[slot]) for slot in range(4)])
    back = back * live_cells[..., None]
    owned = owned.at[cell_ids.reshape(-1)].add(back.reshape(-1, width))
    return tracer_mass + inflow - owned


def solution(mesh):
    placed = (
        P(("groups", "curve"), None),
        P(("groups", "curve"), None),
        P(("groups", "curve")),
        P(("groups", "curve"), None),
        P(("groups", "curve"), None),
        P(None, ("groups", "curve"), None),
    )
    return jax.shard_map(
        local, mesh=mesh, in_specs=placed, out_specs=P(("groups", "curve"), None), check_vma=False
    )
```

profile of v0, /device:TPU:0, one launch (start us, length us, event | category | flops | bytes accessed | tf_op | source)
XLA Modules:
  0.0 111.8 jit_solution(11244870543557881163)
XLA Ops:
  0.0 0.7 broadcast_multiply_fusion.1
  0.7 0.7 fusion.22
  1.5 0.1 add.184
  1.6 0.1 mul.164
  1.8 0.1 add.182
  2.1 3.3 %gather_fusion = f32[1152,200]{1,0:T(8,128)S(1)} fusion(f32[288,200]{1,0:T(8,128)S(1)} %copy-done, s32[2048]{0:T(1024)S(1)} %pad_clamp_fusion), kind=kCustom, calls=%fused_computation | custom fusion | bytes 1847808 | tf_op jit(solution)/shard_map/gather | solution.py:60
  5.4 0.2 broadcast_multiply_fusion
  5.7 0.5 collective-permute-start
  6.2 5.6 %collective-permute-start.3 = (f32[288,200]{1,0:T(8,128)S(1)}, f32[288,200]{1,0:T(8,128)S(1)}, u32[]{:S(2)}, u32[]{:S(2)}) collective-permute-start(f32[288,200]{1,0:T(8,128)S(1)} %get-tuple-element.34), channel_id=1, source_target_pairs={{0,14},{1,15},{2,0},{3,1},{4,2},{5,3},{6,4},{7,5},{8,6},{9,7},{10,... | collective-permute-start | bytes 691208 | tf_op jit(solution)/shard_map/ppermute | solution.py:11
  11.8 1.4 %collective-permute-start.2 = (f32[288,200]{1,0:T(8,128)S(1)}, f32[288,200]{1,0:T(8,128)S(1)}, u32[]{:S(2)}, u32[]{:S(2)}) collective-permute-start(f32[288,200]{1,0:T(8,128)S(1)} %get-tuple-element.35), channel_id=1, source_target_pairs={{0,15},{1,0},{2,1},{3,2},{4,3},{5,4},{6,5},{7,6},{8,7},{9,8},{10,9... | collective-permute-start | bytes 691208 | tf_op jit(solution)/shard_map/ppermute | solution.py:11
  13.3 0.6 pad_clamp_fusion.3
  13.9 0.2 mul.203
  14.1 0.1 concatenate.38
  14.2 0.6 reduce.16
  14.9 0.6 slice_reduce_fusion.11
  15.5 0.6 slice_reduce_fusion.6
  16.1 8.9 %collective-permute-done.3 = f32[288,200]{1,0:T(8,128)S(1)} collective-permute-done((f32[288,200]{1,0:T(8,128)S(1)}, f32[288,200]{1,0:T(8,128)S(1)}, u32[]{:S(2)}, u32[]{:S(2)}) %collective-permute-start.3) | collective-permute-done | bytes 230432 | tf_op jit(solution)/shard_map/ppermute | solution.py:11
  25.0 1.7 %collective-permute-done.1 = f32[288,200]{1,0:T(8,128)S(1)} collective-permute-done((f32[288,200]{1,0:T(8,128)S(1)}, f32[288,200]{1,0:T(8,128)S(1)}, u32[]{:S(2)}, u32[]{:S(2)}) %collective-permute-start.1) | collective-permute-done | bytes 230432 | tf_op jit(solution)/shard_map/ppermute | solution.py:11
  26.8 0.2 fusion.2
  27.1 0.2 fusion
  27.3 0.4 slice-done
  27.8 4.1 %select_select_fusion.1 = (f32[1440,200]{1,0:T(8,128)}, f32[1440,200]{1,0:T(8,128)S(1)}, f32[1440,200]{1,0:T(8,128)S(1)}) fusion(f32[1439,200]{1,0:T(8,128)S(1)} %get-tuple-element.30, f32[1,200]{1,0:T(1,128)S(1)} %slice.194, f32[1,200]{1,0:T(1,128)S(1)} %slice-done, f32[1439,200]{1,0:T(8,128)S(1)} %get-tuple-element.29, ...), kind=kLoop, calls=%fused_computation.33 | loop fusion | flops 4896000 | bytes 9221760 | tf_op jit(solution)/shard_map/jit(_where)/select_n | solution.py:23
  31.9 3.5 %gather_fusion.11 = f32[288,200]{1,0:T(8,128)} fusion(f32[1440,200]{1,0:T(8,128)} %get-tuple-element.26, s32[1024]{0:T(1024)S(1)} %get-tuple-element.43), kind=kCustom, calls=%fused_computation.11 | custom fusion | bytes 461952 | tf_op jit(solution)/shard_map/gather | solution.py:42
  35.4 3.5 %gather_fusion.8 = f32[288,200]{1,0:T(8,128)} fusion(f32[1440,200]{1,0:T(8,128)} %get-tuple-element.26, s32[1024]{0:T(1024)S(1)} %get-tuple-element.44), kind=kCustom, calls=%fused_computation.8 | custom fusion | bytes 461952 | tf_op jit(solution)/shard_map/gather | solution.py:42
  38.9 2.1 %gather_fusion.12 = f32[288,200]{1,0:T(8,128)} fusion(f32[1440,200]{1,0:T(8,128)S(1)} %get-tuple-element.27, s32[1024]{0:T(1024)S(1)} %get-tuple-element.43), kind=kCustom, calls=%fused_computation.12 | custom fusion | bytes 461952 | tf_op jit(solution)/shard_map/gather | solution.py:43
  41.1 2.1 %gather_fusion.9 = f32[288,200]{1,0:T(8,128)} fusion(f32[1440,200]{1,0:T(8,128)S(1)} %get-tuple-element.27, s32[1024]{0:T(1024)S(1)} %get-tuple-element.44), kind=kCustom, calls=%fused_computation.9 | custom fusion | bytes 461952 | tf_op jit(solution)/shard_map/gather | solution.py:43
  43.2 2.1 %gather_fusion.10 = f32[288,200]{1,0:T(8,128)} fusion(f32[1440,200]{1,0:T(8,128)S(1)} %get-tuple-element.28, s32[1024]{0:T(1024)S(1)} %get-tuple-element.43), kind=kCustom, calls=%fused_computation.10 | custom fusion | bytes 461952 | tf_op jit(solution)/shard_map/gather | solution.py:41
  45.3 2.1 %gather_fusion.7 = f32[288,200]{1,0:T(8,128)} fusion(f32[1440,200]{1,0:T(8,128)S(1)} %get-tuple-element.28, s32[1024]{0:T(1024)S(1)} %get-tuple-element.44), kind=kCustom, calls=%fused_computation.7 | custom fusion | bytes 461952 | tf_op jit(solution)/shard_map/gather | solution.py:41
  47.5 3.5 %gather_fusion.5 = f32[288,200]{1,0:T(8,128)} fusion(f32[1440,200]{1,0:T(8,128)} %get-tuple-element.26, s32[1024]{0:T(1024)S(1)} %get-tuple-element.45), kind=kCustom, calls=%fused_computation.5 | custom fusion | bytes 461952 | tf_op jit(solution)/shard_map/gather | solution.py:42
  51.0 2.1 %gather_fusion.6 = f32[288,200]{1,0:T(8,128)} fusion(f32[1440,200]{1,0:T(8,128)S(1)} %get-tuple-element.27, s32[1024]{0:T(1024)S(1)} %get-tuple-element.45), kind=kCustom, calls=%fused_computation.6 | custom fusion | bytes 461952 | tf_op jit(solution)/shard_map/gather | solution.py:43
  53.1 3.0 %gather_fusion.2 = f32[288,200]{1,0:T(8,128)S(1)} fusion(f32[1440,200]{1,0:T(8,128)} %get-tuple-element.26, s32[1024]{0:T(1024)S(1)} %copy-done.11), kind=kCustom, calls=%fused_computation.2 | custom fusion | bytes 461952 | tf_op jit(solution)/shard_map/gather | solution.py:42
  56.1 2.1 %gather_fusion.3 = f32[288,200]{1,0:T(8,128)} fusion(f32[1440,200]{1,0:T(8,128)S(1)} %get-tuple-element.27, s32[1024]{0:T(1024)S(1)} %copy-done.11), kind=kCustom, calls=%fused_computation.3 | custom fusion | bytes 461952 | tf_op jit(solution)/shard_map/gather | solution.py:43
  58.2 2.1 %gather_fusion.1 = f32[288,200]{1,0:T(8,128)} fusion(f32[1440,200]{1,0:T(8,128)S(1)} %get-tuple-element.28, s32[1024]{0:T(1024)S(1)} %copy-done.11), kind=kCustom, calls=%fused_computation.1 | custom fusion | bytes 461952 | tf_op jit(solution)/shard_map/gather | solution.py:41
  60.4 2.1 %gather_fusion.4 = f32[288,200]{1,0:T(8,128)} fusion(f32[1440,200]{1,0:T(8,128)S(1)} %get-tuple-element.28, s32[1024]{0:T(1024)S(1)} %copy-done.10), kind=kCustom, calls=%fused_computation.4 | custom fusion | bytes 461952 | tf_op jit(solution)/shard_map/gather | solution.py:41
  62.7 1.3 %add_multiply_fusion = f32[288,200]{1,0:T(8,128)S(1)} fusion(f32[288,200]{1,0:T(8,128)} %gather_fusion.12, f32[288,200]{1,0:T(8,128)} %gather_fusion.10, f32[288,200]{1,0:T(8,128)S(1)} %copy-done.7, f32[288]{0:T(512)S(1)} %copy-done.21, f32[288]{0:T(512)S(1)} %copy-done.22, f32[288]{0:T(512)S(1)} %copy-done.26), kind=kLoop, calls=%fused_computation.52 | loop fusion | flops 288000 | bytes 925056 | tf_op jit(solution)/shard_map/mul | solution.py:40
  64.1 1.2 %add_multiply_fusion.1 = f32[288,200]{1,0:T(8,128)S(1)} fusion(f32[288,200]{1,0:T(8,128)S(1)} %copy-done.4, f32[288,200]{1,0:T(8,128)} %gather_fusion.7, f32[288,200]{1,0:T(8,128)S(1)} %copy-done.3, f32[288]{0:T(512)S(1)} %copy-done.19, f32[288]{0:T(512)S(1)} %copy-done.20, f32[288]{0:T(512)S(1)} %copy-done.25), kind=kLoop, calls=%fused_computation.53 | loop fusion | flops 288000 | bytes 925056 | tf_op jit(solution)/shard_map/mul | solution.py:40
  65.3 0.2 add_multiply_fusion.2
  65.6 0.2 add_multiply_fusion.3
  65.8 10.3 %scatter_custom_fusion = f32[1440,200]{1,0:T(8,128)S(1)} fusion(s32[1152]{0:T(1024)} %reduce.16, f32[288,200]{1,0:T(8,128)S(1)} %add_multiply_fusion, f32[]{:T(128)} %constant.59, f32[288,200]{1,0:T(8,128)S(1)} %add_multiply_fusion.1, f32[288,200]{1,0:T(8,128)S(1)} %add_multiply_fusion.2, f32[288,200]{1,0:T(8,128)S(1)} %add_multiply_fusion.3, ...), kind=kCustom, calls=%fused_computation.35 | custom fusion | flops 921600 | bytes 2074624 | tf_op jit(solution)/shard_map/add | solution.py:46
  76.0 0.9 fusion.27
  77.0 6.4 %collective-permute-start.4 = (f32[288,200]{1,0:T(8,128)}, f32[288,200]{1,0:T(8,128)S(1)}, u32[]{:S(2)}, u32[]{:S(2)}) collective-permute-start(f32[288,200]{1,0:T(8,128)} %get-tuple-element.21), channel_id=1, source_target_pairs={{0,15},{1,0},{2,1},{3,2},{4,3},{5,4},{6,5},{7,6},{8,7},{9,8},{10,9... | collective-permute-start | bytes 691208 | tf_op jit(solution)/shard_map/ppermute | solution.py:11
  83.4 4.7 %collective-permute-start.5 = (f32[288,200]{1,0:T(8,128)S(1)}, f32[288,200]{1,0:T(8,128)S(1)}, u32[]{:S(2)}, u32[]{:S(2)}) collective-permute-start(f32[288,200]{1,0:T(8,128)S(1)} %get-tuple-element.24), channel_id=1, source_target_pairs={{0,14},{1,15},{2,0},{3,1},{4,2},{5,3},{6,4},{7,5},{8,6},{9,7},{10,... | collective-permute-start | bytes 691208 | tf_op jit(solution)/shard_map/ppermute | solution.py:11
  88.2 0.2 add.210
  88.4 10.2 %collective-permute-done.7 = f32[288,200]{1,0:T(8,128)S(1)} collective-permute-done((f32[288,200]{1,0:T(8,128)}, f32[288,200]{1,0:T(8,128)S(1)}, u32[]{:S(2)}, u32[]{:S(2)}) %collective-permute-start.7) | collective-permute-done | bytes 230432 | tf_op jit(solution)/shard_map/ppermute | solution.py:11
  98.6 3.1 %collective-permute-done.5 = f32[288,200]{1,0:T(8,128)S(1)} collective-permute-done((f32[288,200]{1,0:T(8,128)S(1)}, f32[288,200]{1,0:T(8,128)S(1)}, u32[]{:S(2)}, u32[]{:S(2)}) %collective-permute-start.5) | collective-permute-done | bytes 230432 | tf_op jit(solution)/shard_map/ppermute | solution.py:11
  101.8 0.2 bitcast_multiply_fusion
  102.0 9.0 %scatter_fusion = f32[288,200]{1,0:T(8,128)S(1)} fusion(f32[288,200]{1,0:T(8,128)S(1)} %get-tuple-element.25, s32[1152]{0:T(1024)S(1)} %fusion.21, f32[1152,200]{1,0:T(8,128)S(1)} %bitcast_multiply_fusion), kind=kCustom, calls=%fused_computation.14 | custom fusion | flops 230400 | bytes 2769408 | tf_op jit(solution)/shard_map/scatter-add | solution.py:68
  111.0 0.8 add_subtract_fusion
  (86 shorter events, 0.9 us)
Async XLA Ops:
  0.0 2.1 %copy-start = (f32[288,200]{1,0:T(8,128)S(1)}, f32[288,200]{1,0:T(8,128)}, u32[]{:S(2)}) copy-start(f32[288,200]{1,0:T(8,128)} %param.6) | copy-start | bytes 691204
  0.7 1.3 %copy-start.12 = (s32[4,32]{1,0:T(4,128)}, s32[4,32]{1,0:T(4,128)S(1)}, u32[]{:S(2)}) copy-start(s32[4,32]{1,0:T(4,128)S(1)} %broadcast_multiply_fusion.1) | copy-start | bytes 1540
  5.6 7.6 %copy-start.14 = (f32[2,288,4]{1,2,0:T(4,128)S(1)}, f32[2,288,4]{1,2,0:T(4,128)}, u32[]{:S(2)}) copy-start(f32[2,288,4]{1,2,0:T(4,128)} %param.11) | copy-start | bytes 27652
  5.6 7.7 %copy-start.28 = (s32[288,4]{0,1:T(4,128)S(1)}, s32[288,4]{0,1:T(4,128)}, u32[]{:S(2)}) copy-start(s32[288,4]{0,1:T(4,128)} %param.9) | copy-start | bytes 13828
  5.6 9.2 %copy-start.27 = (f32[288,4]{0,1:T(4,128)S(1)}, f32[288,4]{0,1:T(4,128)}, u32[]{:S(2)}) copy-start(f32[288,4]{0,1:T(4,128)} %param.10) | copy-start | bytes 13828
  5.7 10.4 %collective-permute-start = (f32[288,200]{1,0:T(8,128)S(1)}, f32[288,200]{1,0:T(8,128)S(1)}, u32[]{:S(2)}, u32[]{:S(2)}) collective-permute-start(f32[288,200]{1,0:T(8,128)S(1)} %get-tuple-element.33), channel_id=1, source_target_pairs={{0,1},{1,2},{2,3},{3,4},{4,5},{5,6},{6,7},{7,8},{8,9},{9,10},{10,1... | collective-permute-start | bytes 691208 | tf_op jit(solution)/shard_map/ppermute | solution.py:11
  6.2 18.8 %collective-permute-start.3 = (f32[288,200]{1,0:T(8,128)S(1)}, f32[288,200]{1,0:T(8,128)S(1)}, u32[]{:S(2)}, u32[]{:S(2)}) collective-permute-start(f32[288,200]{1,0:T(8,128)S(1)} %get-tuple-element.34), channel_id=1, source_target_pairs={{0,14},{1,15},{2,0},{3,1},{4,2},{5,3},{6,4},{7,5},{8,6},{9,7},{10,... | collective-permute-start | bytes 691208 | tf_op jit(solution)/shard_map/ppermute | solution.py:11
  11.8 13.2 %collective-permute-start.2 = (f32[288,200]{1,0:T(8,128)S(1)}, f32[288,200]{1,0:T(8,128)S(1)}, u32[]{:S(2)}, u32[]{:S(2)}) collective-permute-start(f32[288,200]{1,0:T(8,128)S(1)} %get-tuple-element.35), channel_id=1, source_target_pairs={{0,15},{1,0},{2,1},{3,2},{4,3},{5,4},{6,5},{7,6},{8,7},{9,8},{10,9... | collective-permute-start | bytes 691208 | tf_op jit(solution)/shard_map/ppermute | solution.py:11
  13.2 13.5 %collective-permute-start.1 = (f32[288,200]{1,0:T(8,128)S(1)}, f32[288,200]{1,0:T(8,128)S(1)}, u32[]{:S(2)}, u32[]{:S(2)}) collective-permute-start(f32[288,200]{1,0:T(8,128)S(1)} %get-tuple-element.36), channel_id=1, source_target_pairs={{0,2},{1,3},{2,4},{3,5},{4,6},{5,7},{6,8},{7,9},{8,10},{9,11},{10,... | collective-permute-start | bytes 691208 | tf_op jit(solution)/shard_map/ppermute | solution.py:11
  13.9 37.1 %copy-start.9 = (s32[1024]{0:T(1024)}, s32[1024]{0:T(1024)S(1)}, u32[]{:S(2)}) copy-start(s32[1024]{0:T(1024)S(1)} %get-tuple-element.45) | copy-start | bytes 12292
  27.0 0.7 slice-start
  27.1 0.7 slice-start.1
  51.0 2.1 %copy-start.11 = (s32[1024]{0:T(1024)S(1)}, s32[1024]{0:T(1024)}, u32[]{:S(2)}) copy-start(s32[1024]{0:T(1024)} %get-tuple-element.46) | copy-start | bytes 12292
  58.2 2.1 %copy-start.10 = (s32[1024]{0:T(1024)S(1)}, s32[1024]{0:T(1024)}, u32[]{:S(2)}) copy-start(s32[1024]{0:T(1024)} %copy-done.9) | copy-start | bytes 12292
  60.4 2.2 %copy-start.7 = (f32[288,200]{1,0:T(8,128)S(1)}, f32[288,200]{1,0:T(8,128)}, u32[]{:S(2)}) copy-start(f32[288,200]{1,0:T(8,128)} %gather_fusion.11) | copy-start | bytes 691204
  60.4 2.3 %copy-start.21 = (f32[288]{0:T(512)S(1)}, f32[288]{0:T(512)}, u32[]{:S(2)}) copy-start(f32[288]{0:T(512)} %get-tuple-element.14) | copy-start | bytes 3460
  60.4 2.3 %copy-start.22 = (f32[288]{0:T(512)S(1)}, f32[288]{0:T(512)}, u32[]{:S(2)}) copy-start(f32[288]{0:T(512)} %get-tuple-element.53) | copy-start | bytes 3460
  60.4 2.3 %copy-start.26 = (f32[288]{0:T(512)S(1)}, f32[288]{0:T(512)}, u32[]{:S(2)}) copy-start(f32[288]{0:T(512)} %get-tuple-element.7) | copy-start | bytes 3460
  60.4 3.6 %copy-start.3 = (f32[288,200]{1,0:T(8,128)S(1)}, f32[288,200]{1,0:T(8,128)}, u32[]{:S(2)}) copy-start(f32[288,200]{1,0:T(8,128)} %gather_fusion.8) | copy-start | bytes 691204
  60.4 3.6 %copy-start.4 = (f32[288,200]{1,0:T(8,128)S(1)}, f32[288,200]{1,0:T(8,128)}, u32[]{:S(2)}) copy-start(f32[288,200]{1,0:T(8,128)} %gather_fusion.9) | copy-start | bytes 691204
  60.4 3.6 %copy-start.19 = (f32[288]{0:T(512)S(1)}, f32[288]{0:T(512)}, u32[]{:S(2)}) copy-start(f32[288]{0:T(512)} %get-tuple-element.15) | copy-start | bytes 3460
  60.4 3.6 %copy-start.20 = (f32[288]{0:T(512)S(1)}, f32[288]{0:T(512)}, u32[]{:S(2)}) copy-start(f32[288]{0:T(512)} %get-tuple-element.52) | copy-start | bytes 3460
  60.4 3.6 %copy-start.25 = (f32[288]{0:T(512)S(1)}, f32[288]{0:T(512)}, u32[]{:S(2)}) copy-start(f32[288]{0:T(512)} %get-tuple-element.8) | copy-start | bytes 3460
  62.6 2.7 %copy-start.5 = (f32[288,200]{1,0:T(8,128)S(1)}, f32[288,200]{1,0:T(8,128)}, u32[]{:S(2)}) copy-start(f32[288,200]{1,0:T(8,128)} %gather_fusion.5) | copy-start | bytes 691204
  62.6 2.7 %copy-start.6 = (f32[288,200]{1,0:T(8,128)S(1)}, f32[288,200]{1,0:T(8,128)}, u32[]{:S(2)}) copy-start(f32[288,200]{1,0:T(8,128)} %gather_fusion.6) | copy-start | bytes 691204
  62.6 2.7 %copy-start.8 = (f32[288,200]{1,0:T(8,128)S(1)}, f32[288,200]{1,0:T(8,128)}, u32[]{:S(2)}) copy-start(f32[288,200]{1,0:T(8,128)} %gather_fusion.4) | copy-start | bytes 691204
  62.6 2.7 %copy-start.17 = (f32[288]{0:T(512)S(1)}, f32[288]{0:T(512)}, u32[]{:S(2)}) copy-start(f32[288]{0:T(512)} %get-tuple-element.16) | copy-start | bytes 3460
  62.6 2.7 %copy-start.18 = (f32[288]{0:T(512)S(1)}, f32[288]{0:T(512)}, u32[]{:S(2)}) copy-start(f32[288]{0:T(512)} %get-tuple-element.51) | copy-start | bytes 3460
  62.6 2.7 %copy-start.24 = (f32[288]{0:T(512)S(1)}, f32[288]{0:T(512)}, u32[]{:S(2)}) copy-start(f32[288]{0:T(512)} %get-tuple-element.6) | copy-start | bytes 3460
  64.0 1.6 %copy-start.1 = (f32[288,200]{1,0:T(8,128)S(1)}, f32[288,200]{1,0:T(8,128)}, u32[]{:S(2)}) copy-start(f32[288,200]{1,0:T(8,128)} %gather_fusion.3) | copy-start | bytes 691204
  64.0 1.6 %copy-start.2 = (f32[288,200]{1,0:T(8,128)S(1)}, f32[288,200]{1,0:T(8,128)}, u32[]{:S(2)}) copy-start(f32[288,200]{1,0:T(8,128)} %gather_fusion.1) | copy-start | bytes 691204
  64.0 1.6 %copy-start.15 = (f32[288]{0:T(512)S(1)}, f32[288]{0:T(512)}, u32[]{:S(2)}) copy-start(f32[288]{0:T(512)} %get-tuple-element.13) | copy-start | bytes 3460
  64.0 1.6 %copy-start.16 = (f32[288]{0:T(512)S(1)}, f32[288]{0:T(512)}, u32[]{:S(2)}) copy-start(f32[288]{0:T(512)} %get-tuple-element.54) | copy-start | bytes 3460
  64.0 1.6 %copy-start.23 = (f32[288]{0:T(512)S(1)}, f32[288]{0:T(512)}, u32[]{:S(2)}) copy-start(f32[288]{0:T(512)} %get-tuple-element.5) | copy-start | bytes 3460
  76.0 12.1 %copy-start.13 = (s32[4,32]{1,0:T(4,128)S(1)}, s32[4,32]{1,0:T(4,128)}, u32[]{:S(2)}) copy-start(s32[4,32]{1,0:T(4,128)} %copy-done.12) | copy-start | bytes 1540
  77.0 11.5 %collective-permute-start.4 = (f32[288,200]{1,0:T(8,128)}, f32[288,200]{1,0:T(8,128)S(1)}, u32[]{:S(2)}, u32[]{:S(2)}) collective-permute-start(f32[288,200]{1,0:T(8,128)} %get-tuple-element.21), channel_id=1, source_target_pairs={{0,15},{1,0},{2,1},{3,2},{4,3},{5,4},{6,5},{7,6},{8,7},{9,8},{10,9... | collective-permute-start | bytes 691208 | tf_op jit(solution)/shard_map/ppermute | solution.py:11
  83.4 15.2 %collective-permute-start.7 = (f32[288,200]{1,0:T(8,128)}, f32[288,200]{1,0:T(8,128)S(1)}, u32[]{:S(2)}, u32[]{:S(2)}) collective-permute-start(f32[288,200]{1,0:T(8,128)} %get-tuple-element.22), channel_id=1, source_target_pairs={{0,2},{1,3},{2,4},{3,5},{4,6},{5,7},{6,8},{7,9},{8,10},{9,11},{10,... | collective-permute-start | bytes 691208 | tf_op jit(solution)/shard_map/ppermute | solution.py:11
  83.4 15.2 %collective-permute-start.6 = (f32[288,200]{1,0:T(8,128)}, f32[288,200]{1,0:T(8,128)S(1)}, u32[]{:S(2)}, u32[]{:S(2)}) collective-permute-start(f32[288,200]{1,0:T(8,128)} %get-tuple-element.23), channel_id=1, source_target_pairs={{0,1},{1,2},{2,3},{3,4},{4,5},{5,6},{6,7},{7,8},{8,9},{9,10},{10,1... | collective-permute-start | bytes 691208 | tf_op jit(solution)/shard_map/ppermute | solution.py:11
  83.4 18.3 %collective-permute-start.5 = (f32[288,200]{1,0:T(8,128)S(1)}, f32[288,200]{1,0:T(8,128)S(1)}, u32[]{:S(2)}, u32[]{:S(2)}) collective-permute-start(f32[288,200]{1,0:T(8,128)S(1)} %get-tuple-element.24), channel_id=1, source_target_pairs={{0,14},{1,15},{2,0},{3,1},{4,2},{5,3},{6,4},{7,5},{8,6},{9,7},{10,... | collective-permute-start | bytes 691208 | tf_op jit(solution)/shard_map/ppermute | solution.py:11
where the time goes:
time: 112 us
  local copies, waits for them, and re-layouts  37.8 us (34%)
  other arithmetic  30.9 us (28%)
  waiting for transfers between devices  23.9 us (21%)
  starting transfers between devices  18.6 us (17%)
    ppermute x8, waiting for transfers between devices, from_behind(): return lax.ppermute(x, axis, [(i, (i + by) % count) for i in range(count)])  23.9 us
    ppermute x8, starting transfers between devices, from_behind(): return lax.ppermute(x, axis, [(i, (i + by) % count) for i in range(count)])  18.6 us
    gather x4, local copies, waits for them, and re-layouts, transport(): slope_x[source]  13.5 us
    add x1, other arithmetic, transport(): outflow + jax.ops.segment_sum(flux, source, num_segments=total_cells)  10.3 us
    scatter-add x1, other arithmetic, local(): owned = owned.at[cell_ids.reshape(-1)].add(back.reshape(-1, width))  9.01 us
    gather x4, local copies, waits for them, and re-layouts, transport(): slope_y[source]  8.54 us
    gather x4, local copies, waits for them, and re-layouts, transport(): extended[source] + moment_x[:, column, None] * slope_x[source]  8.53 us
    select_n x1, other arithmetic, build_slopes(): jnp.where(column == 0, right - values, jnp.where(column == 1, 0.5 * (righ...  4.12 us
  transfers between devices with their start and end apart: 8, of which 4 were waited for; matrix products, arithmetic and copies ran while one was open for 3% of the time, Pallas kernels for 0%

commit v1 on v0

v1 whole, which is shorter than its diff:
```python
import functools

import jax
import jax.numpy as jnp
from jax import lax
from jax.experimental import pallas as pl
from jax.experimental.pallas import tpu as pltpu
from jax.sharding import PartitionSpec as P

OFFSETS = (1, 2, -1, -2)
ORDER = (1, 3, 0, 2)
LANES = 128
CHUNK = 32
F32 = jnp.float32
BF16 = jnp.bfloat16


def round_up(value, unit):
    return -(-value // unit) * unit


def iota(shape, axis):
    return lax.broadcasted_iota(jnp.int32, shape, axis)


def ninth(value):
    return lax.shift_right_logical(value * 7282, 16)


def dot(a, b):
    return jnp.dot(a, b, preferred_element_type=F32)


def split(value):
    high = value.astype(BF16)
    return high, (value - high.astype(F32)).astype(BF16)


def difference_matrix(size, cells, stride):
    row, col = iota((size, size), 0), iota((size, size), 1)
    step = row if stride == 1 else (row * 21846) >> 16
    place = step - 3 * ((step * 21846) >> 16)
    delta = col - row
    first = jnp.where(delta == stride, 1.0, jnp.where(delta == 0, -1.0, 0.0))
    middle = jnp.where(delta == stride, 0.5, jnp.where(delta == -stride, -0.5, 0.0))
    last = jnp.where(delta == 0, 1.0, jnp.where(delta == -stride, -1.0, 0.0))
    value = jnp.where(place == 0, first, jnp.where(place == 1, middle, last))
    return jnp.where((row < cells) & (col < cells), value, 0.0).astype(BF16)


def kernel(
    count, mass_hbm, ids_ref, counts_ref, src_ref, frac_ref, mom_ref, out_ref,
    own, got, enc, enc_got, coef, coef_got, rows, cols, wq, wx, wy, high, low, dx, dy,
    own_sem, mass_send, mass_recv, enc_send, enc_recv, coef_send, coef_recv,
):
    cells, width = own.shape
    lists, slots = ids_ref.shape
    pieces = src_ref.shape[0]
    size = wq.shape[1]
    own_elements = cells // 9
    block = round_up(size, 512)
    me = lax.axis_index("curve")

    def at(offset):
        return {"curve": lax.rem(me + offset + count, count)}

    local = pltpu.make_async_copy(mass_hbm, own, own_sem)
    local.start()

    barrier = pltpu.get_barrier_semaphore()
    for offset in OFFSETS:
        pl.semaphore_signal(
            barrier, inc=1, device_id=at(offset), device_id_type=pl.DeviceIdType.MESH
        )

    wide = jnp.concatenate([ids_ref[...]] * lists, axis=1)
    row, lane = iota(wide.shape, 0), iota(wide.shape, 1)
    slot = lane - row * slots
    live = jnp.zeros(wide.shape, jnp.int32)
    for o in range(lists):
        live = jnp.where(row == o, counts_ref[o], live)
    keep = (slot >= 0) & (slot < slots) & (slot < live)
    enc[...] = jnp.zeros(enc.shape, F32)
    enc[0:lists, :] = jnp.where(keep, wide + 1, 0).astype(F32)

    pl.semaphore_wait(barrier, len(OFFSETS))

    def remote(src, dst, send, recv, o, offset):
        return pltpu.make_async_remote_copy(
            src_ref=src, dst_ref=dst, send_sem=send.at[o], recv_sem=recv.at[o],
            device_id=at(offset), device_id_type=pl.DeviceIdType.MESH,
        )

    enc_copy = [
        remote(enc, enc_got.at[o], enc_send, enc_recv, o, OFFSETS[o]) for o in range(lists)
    ]
    mass_copy = [
        remote(mass_hbm, got.at[o], mass_send, mass_recv, o, OFFSETS[o]) for o in range(lists)
    ]
    coef_copy = [
        remote(coef.at[o + 1], coef_got.at[o], coef_send, coef_recv, o, -OFFSETS[o])
        for o in range(lists)
    ]
    for o in ORDER:
        enc_copy[o].start()
    for o in ORDER:
        mass_copy[o].start()

    dx[...] = difference_matrix(size, cells, 1)
    dy[...] = difference_matrix(size, cells, 3)
    rows[...] = jnp.zeros(rows.shape, F32)
    src = src_ref[...]
    element = ninth(src)
    inside = src - 9 * element
    frac = frac_ref[...]
    rows[8 : 8 + pieces, 0:cells] = frac
    rows[16 : 16 + pieces, 0:cells] = frac * mom_ref[0]
    rows[24 : 24 + pieces, 0:cells] = frac * mom_ref[1]

    for o in ORDER:
        enc_copy[o].wait_recv()
    table = jnp.zeros((1, lists * slots), F32)
    for o in range(lists):
        table = table + enc_got[o, o : o + 1, :]
    table = jnp.broadcast_to(table, (16, lists * slots)).astype(BF16)
    for k in range(pieces):
        e = element[k : k + 1, :]
        hit = iota((lists * slots, cells), 0) + own_elements == e
        found = dot(table, jnp.where(hit, 1.0, 0.0).astype(BF16))[0:1, :]
        part = jnp.ones(e.shape, jnp.int32)
        for o in range(1, lists):
            part = part + jnp.where(e >= own_elements + o * slots, 1, 0)
        moved = (block * part + inside[k : k + 1, :]).astype(F32) + 9.0 * (found - 1.0)
        rows[k : k + 1, 0:cells] = jnp.where(
            e < own_elements, src[k : k + 1, :].astype(F32), jnp.where(found > 0.5, moved, -1.0)
        )
    cols[...] = rows[...].T

    def build(o):
        lane_id = (iota((CHUNK, size), 1) + o * block).astype(F32)

        def step(i, sums):
            at_rows = pl.ds(pl.multiple_of(i * CHUNK, CHUNK), CHUNK)
            q = jnp.zeros((CHUNK, size), F32)
            x, y = q, q
            for k in range(pieces):
                hit = lane_id == cols[at_rows, k : k + 1]
                q = q + jnp.where(hit, cols[at_rows, 8 + k : 9 + k], 0.0)
                x = x + jnp.where(hit, cols[at_rows, 16 + k : 17 + k], 0.0)
                y = y + jnp.where(hit, cols[at_rows, 24 + k : 25 + k], 0.0)
            wq[at_rows, :] = q
            wx[at_rows, :] = x
            wy[at_rows, :] = y
            return tuple(
                s + v.reshape(CHUNK // 8, 8, size).sum(0) for s, v in zip(sums, (q, x, y))
            )

        zero = jnp.zeros((8, size), F32)
        sums = lax.fori_loop(0, cells // CHUNK, step, (zero, zero, zero))
        for j in range(3):
            coef[o, j : j + 1, :] = jnp.sum(sums[j], axis=0, keepdims=True)

    def fold(o):
        xh, xl = split(wx[...])
        yh, yl = split(wy[...])
        ddx, ddy = dx[...], dy[...]
        total = wq[...] + dot(xh, ddx) + dot(xl, ddx) + dot(yh, ddy) + dot(yl, ddy)
        h, l = split(total)
        high[o] = h
        low[o] = l

    def apply(o, value):
        vh, vl = split(value)
        h, l = high[o, :, 0:cells], low[o, :, 0:cells]
        return dot(h, vh) + dot(h, vl) + dot(l, vh)

    for o in range(lists):
        coef[o + 1] = jnp.zeros((8, size), F32)
        build(o + 1)
        coef_copy[o].start()
        fold(o + 1)

    build(0)
    for o in range(lists):
        coef_copy[o].wait_recv()
    diagonal = iota((cells, size), 0) == iota((cells, size), 1)
    for j, w in enumerate((wq, wx, wy)):
        total = coef[0, j : j + 1, :]
        for o in range(lists):
            total = total + coef_got[o, j : j + 1, :]
        w[...] = w[...] - jnp.where(diagonal, total, 0.0)
    fold(0)
    local.wait()
    mass = own[...]
    out_ref[...] = mass + apply(0, mass)
    for o in (2, 0, 3, 1):
        mass_copy[o].wait_recv()
        out_ref[...] += apply(o + 1, got[o])
    for o in range(lists):
        enc_copy[o].wait_send()
        mass_copy[o].wait_send()
        coef_copy[o].wait_send()


def local(mesh, tracer_mass, send_ids, send_counts, sources, fractions, moments):
    cells, width = tracer_mass.shape
    lists, slots = send_ids.shape
    size = round_up(cells, LANES)
    vmem = pl.BlockSpec(memory_space=pltpu.VMEM)
    dma = pltpu.SemaphoreType.DMA
    return pl.pallas_call(
        functools.partial(kernel, mesh.shape["curve"]),
        out_shape=jax.ShapeDtypeStruct((cells, width), F32),
        in_specs=[
            pl.BlockSpec(memory_space=pl.ANY),
            vmem,
            pl.BlockSpec(memory_space=pltpu.SMEM),
            vmem,
            vmem,
            vmem,
        ],
        out_specs=vmem,
        scratch_shapes=[
            pltpu.VMEM((cells, width), F32),
            pltpu.VMEM((lists, cells, width), F32),
            pltpu.VMEM((8, lists * slots), F32),
            pltpu.VMEM((lists, 8, lists * slots), F32),
            pltpu.VMEM((lists + 1, 8, size), F32),
            pltpu.VMEM((lists, 8, size), F32),
            pltpu.VMEM((LANES, size), F32),
            pltpu.VMEM((size, LANES), F32),
            pltpu.VMEM((cells, size), F32),
            pltpu.VMEM((cells, size), F32),
            pltpu.VMEM((cells, size), F32),
            pltpu.VMEM((lists + 1, cells, size), BF16),
            pltpu.VMEM((lists + 1, cells, size), BF16),
            pltpu.VMEM((size, size), BF16),
            pltpu.VMEM((size, size), BF16),
            dma,
        ]
        + [dma((lists,))] * 6,
        compiler_params=pltpu.CompilerParams(
            collective_id=0, has_side_effects=True, vmem_limit_bytes=40 * 2**20
        ),
        name="transport",
    )(tracer_mass, send_ids, send_counts, sources.T, fractions.T, moments.transpose(0, 2, 1))


def solution(mesh):
    placed = (
        P(("groups", "curve"), None),
        P(("groups", "curve"), None),
        P(("groups", "curve")),
        P(("groups", "curve"), None),
        P(("groups", "curve"), None),
        P(None, ("groups", "curve"), None),
    )
    return jax.shard_map(
        functools.partial(local, mesh),
        mesh=mesh, in_specs=placed, out_specs=P(("groups", "curve"), None), check_vma=False,
    )
```

time: 112 us -> 35.3 us (0.32)
  local copies, waits for them, and re-layouts: 37.8 us -> 4.45 us
  other arithmetic: 30.9 us -> 0 us
  Pallas kernels: 0 us -> 30.2 us
  waiting for transfers between devices: 23.9 us -> 0 us
  starting transfers between devices: 18.6 us -> 0 us
    gather x13 -> x0, local copies, waits for them, and re-layouts: 33.8 us -> none  [the longest x4 13.5 us: transport(): slope_x[source]]
    pallas_call x0 -> x1, Pallas kernels: none -> 30.2 us  [local(): pl.pallas_call(functools.partial(kernel, mesh.shape['curve']), out_shape=...]
    ppermute x8 -> x0, waiting for transfers between devices: 23.9 us -> none  [from_behind(): return lax.ppermute(x, axis, [(i, (i + by) % count) for i in range(count)])]
    ppermute x8 -> x0, starting transfers between devices: 18.6 us -> none  [from_behind(): return lax.ppermute(x, axis, [(i, (i + by) % count) for i in range(count)])]
    add x2 -> x0, other arithmetic: 10.3 us -> none  [the longest x1 10.3 us: transport(): outflow + jax.ops.segment_sum(flux, source, num_segments=total_cells)]
    scatter-add x1 -> x0, other arithmetic: 9.01 us -> none  [local(): owned = owned.at[cell_ids.reshape(-1)].add(back.reshape(-1, width))]
    unnamed x58 -> x13, local copies, waits for them, and re-layouts: 0.12 us -> 4.45 us
    select_n x4 -> x0, other arithmetic: 4.19 us -> none  [the longest x1 4.12 us: build_slopes(): jnp.where(column == 0, right - values, jnp.where(column == 1, 0.5 * (righ...]
  transfers between devices with their start and end apart: 8 -> 0, of which waited for: 4 -> 0; matrix products, arithmetic and copies ran while one was open for 3% -> 0% of each run, Pallas kernels for 0% -> 0%
where the time goes in v1:
time: 35.3 us; the launch traced here: 34.6 us
  Pallas kernels  30.2 us (86%)
  local copies, waits for them, and re-layouts  4.45 us (13%)
    pallas_call x1, Pallas kernels, local(): pl.pallas_call(functools.partial(kernel, mesh.shape['curve']), out_shape=...  30.2 us
    unnamed x13, local copies, waits for them, and re-layouts  4.45 us

profile of v1, /device:TPU:0, one launch (start us, length us, event | category | flops | bytes accessed | tf_op | source)
XLA Modules:
  0.0 34.6 jit_solution(9712901633428040269)
XLA Ops:
  0.0 0.0 copy-start.4
  0.0 0.0 copy-start.5
  0.0 0.7 %copy-done.4 = s32[4,32]{1,0:T(4,128)S(1)} copy-done((s32[4,32]{1,0:T(4,128)S(1)}, s32[4,32]{1,0:T(4,128)}, u32[]{:S(2)}) %copy-start.4) | copy-done | bytes 536
  0.7 0.0 copy-done.5
  0.7 0.0 copy-start
  0.7 1.0 %copy-done = f32[288,200]{1,0:T(8,128)S(1)} copy-done((f32[288,200]{1,0:T(8,128)S(1)}, f32[288,200]{1,0:T(8,128)}, u32[]{:S(2)}) %copy-start) | copy-done | bytes 230424
  1.6 0.0 copy-start.1
  1.6 0.7 %copy-done.1 = f32[2,288,4]{1,2,0:T(4,128)S(1)} copy-done((f32[2,288,4]{1,2,0:T(4,128)S(1)}, f32[2,288,4]{1,2,0:T(4,128)}, u32[]{:S(2)}) %copy-start.1) | copy-done | bytes 9240
  2.4 0.0 copy-start.2
  2.4 0.7 %copy-done.2 = s32[288,4]{0,1:T(4,128)S(1)} copy-done((s32[288,4]{0,1:T(4,128)S(1)}, s32[288,4]{0,1:T(4,128)}, u32[]{:S(2)}) %copy-start.2) | copy-done | bytes 4632
  3.0 0.0 copy-start.3
  3.0 0.7 %copy-done.3 = f32[288,4]{0,1:T(4,128)S(1)} copy-done((f32[288,4]{0,1:T(4,128)S(1)}, f32[288,4]{0,1:T(4,128)}, u32[]{:S(2)}) %copy-start.3) | copy-done | bytes 4632
  3.7 30.2 %transport.1 = f32[288,200]{1,0:T(8,128)S(1)} custom-call(f32[288,200]{1,0:T(8,128)S(1)} %copy-done, s32[4,32]{1,0:T(4,128)S(1)} %copy-done.4, s32[4]{0:T(128)S(1)} %copy-done.5, s32[4,288]{1,0:T(4,128)S(1)} %bitcast.4, f32[4,288]{1,0:T(4,128)S(1)} %bitcast.5, f32[2,4,288]{2,1,0:T(4,128)S(1)} %bitcast.3), custom_call_target="tpu_custom_call" | custom-call | tf_op jit(solution)/shard_map/transport/pallas_call | solution.py:211
  33.9 0.7 %copy.8 = f32[288,200]{1,0:T(8,128)} copy(f32[288,200]{1,0:T(8,128)S(1)} %transport.1) | data formatting | bytes 460800
Async XLA Ops:
  0.0 0.7 %copy-start.4 = (s32[4,32]{1,0:T(4,128)S(1)}, s32[4,32]{1,0:T(4,128)}, u32[]{:S(2)}) copy-start(s32[4,32]{1,0:T(4,128)} %ids_ref.1) | copy-start | bytes 1540
  0.0 0.7 %copy-start.5 = (s32[4]{0:T(128)S(1)}, s32[4]{0:T(128)}, u32[]{:S(2)}) copy-start(s32[4]{0:T(128)} %counts_ref.1) | copy-start | bytes 52
  0.7 1.0 %copy-start = (f32[288,200]{1,0:T(8,128)S(1)}, f32[288,200]{1,0:T(8,128)}, u32[]{:S(2)}) copy-start(f32[288,200]{1,0:T(8,128)} %mass_hbm.1) | copy-start | bytes 691204
  1.6 0.7 %copy-start.1 = (f32[2,288,4]{1,2,0:T(4,128)S(1)}, f32[2,288,4]{1,2,0:T(4,128)}, u32[]{:S(2)}) copy-start(f32[2,288,4]{1,2,0:T(4,128)} %param.11) | copy-start | bytes 27652
  2.4 0.7 %copy-start.2 = (s32[288,4]{0,1:T(4,128)S(1)}, s32[288,4]{0,1:T(4,128)}, u32[]{:S(2)}) copy-start(s32[288,4]{0,1:T(4,128)} %param.9) | copy-start | bytes 13828
  3.0 0.7 %copy-start.3 = (f32[288,4]{0,1:T(4,128)S(1)}, f32[288,4]{0,1:T(4,128)}, u32[]{:S(2)}) copy-start(f32[288,4]{0,1:T(4,128)} %param.10) | copy-start | bytes 13828

commit v2 on v1

--- a/solution.py
+++ b/solution.py
@@ -11,6 +11,7 @@
 ORDER = (1, 3, 0, 2)
 LANES = 128
 CHUNK = 32
+PARTS = 3
 F32 = jnp.float32
 BF16 = jnp.bfloat16
 
@@ -49,9 +50,10 @@
 
 
 def kernel(
-    count, mass_hbm, ids_ref, counts_ref, src_ref, frac_ref, mom_ref, out_ref,
-    own, got, enc, enc_got, coef, coef_got, rows, cols, wq, wx, wy, high, low, dx, dy,
-    own_sem, mass_send, mass_recv, enc_send, enc_recv, coef_send, coef_recv,
+    count, mass_hbm, ids_hbm, counts_hbm, src_hbm, frac_hbm, mom_hbm, out_ref,
+    own, ids_ref, counts_ref, src_ref, frac_ref, mom_ref,
+    got, enc, enc_got, coef, coef_got, rows, cols, wq, wx, wy, high, low, dx, dy, sx, sy,
+    in_sem, mass_send, mass_recv, enc_send, enc_recv, coef_send, coef_recv,
 ):
     cells, width = own.shape
     lists, slots = ids_ref.shape
@@ -64,14 +66,27 @@
     def at(offset):
         return {"curve": lax.rem(me + offset + count, count)}
 
-    local = pltpu.make_async_copy(mass_hbm, own, own_sem)
-    local.start()
+    core = lax.rem(me, 2)
+    odd = lax.rem(lax.div(me, 2), 2)
+    sign = 1 - 2 * odd
 
     barrier = pltpu.get_barrier_semaphore()
-    for offset in OFFSETS:
+    for offset in OFFSETS + (4, -4):
         pl.semaphore_signal(
             barrier, inc=1, device_id=at(offset), device_id_type=pl.DeviceIdType.MESH
         )
+
+    inputs = [
+        pltpu.make_async_copy(a, b, in_sem.at[j])
+        for j, (a, b) in enumerate((
+            (ids_hbm, ids_ref), (counts_hbm, counts_ref), (src_hbm, src_ref),
+            (frac_hbm, frac_ref), (mom_hbm, mom_ref), (mass_hbm, own),
+        ))
+    ]
+    for copy in inputs:
+        copy.start()
+    inputs[0].wait()
+    inputs[1].wait()
 
     wide = jnp.concatenate([ids_ref[...]] * lists, axis=1)
     row, lane = iota(wide.shape, 0), iota(wide.shape, 1)
@@ -83,7 +98,7 @@
     enc[...] = jnp.zeros(enc.shape, F32)
     enc[0:lists, :] = jnp.where(keep, wide + 1, 0).astype(F32)
 
-    pl.semaphore_wait(barrier, len(OFFSETS))
+    pl.semaphore_wait(barrier, len(OFFSETS) + 2)
 
     def remote(src, dst, send, recv, o, offset):
         return pltpu.make_async_remote_copy(
@@ -94,21 +109,44 @@
     enc_copy = [
         remote(enc, enc_got.at[o], enc_send, enc_recv, o, OFFSETS[o]) for o in range(lists)
     ]
-    mass_copy = [
-        remote(mass_hbm, got.at[o], mass_send, mass_recv, o, OFFSETS[o]) for o in range(lists)
-    ]
+    depth = cells // PARTS
+
+    def pass_on(slot, src, offset):
+        return [
+            remote(
+                src.at[pl.ds(j * depth, depth)], got.at[slot, pl.ds(j * depth, depth)],
+                mass_send, mass_recv, slot * PARTS + j, offset,
+            )
+            for j in range(PARTS)
+        ]
+
+    shared = lax.rem(core + odd, 2)
+    near = pass_on(0, mass_hbm, 2 * sign)
+    far = pass_on(1, got.at[0], 4 * sign)
+    sibling = pass_on(2, mass_hbm, 1 - 2 * core)
+    share = pass_on(3, got.at[shared], 1 - 2 * core)
     coef_copy = [
         remote(coef.at[o + 1], coef_got.at[o], coef_send, coef_recv, o, -OFFSETS[o])
         for o in range(lists)
     ]
     for o in ORDER:
         enc_copy[o].start()
-    for o in ORDER:
-        mass_copy[o].start()
+    for copy in near + sibling:
+        copy.start()
+
+    def forward(j):
+        near[j].wait_recv()
+        far[j].start()
+
+    def hand_over(j):
+        far[j].wait_recv()
+        share[j].start()
 
     dx[...] = difference_matrix(size, cells, 1)
     dy[...] = difference_matrix(size, cells, 3)
     rows[...] = jnp.zeros(rows.shape, F32)
+    for copy in inputs[2:5]:
+        copy.wait()
     src = src_ref[...]
     element = ninth(src)
     inside = src - 9 * element
@@ -178,50 +216,65 @@
         coef[o + 1] = jnp.zeros((8, size), F32)
         build(o + 1)
         coef_copy[o].start()
+        if o < PARTS:
+            forward(o)
         fold(o + 1)
-
+    hand_over(0)
+
+    coef[0] = jnp.zeros((8, size), F32)
     build(0)
+    fold(0)
+    hand_over(1)
+    inputs[5].wait()
+    mass = own[...]
+    vh, vl = split(mass)
+    ddx, ddy = dx[0:cells, 0:cells], dy[0:cells, 0:cells]
+    sx[...] = dot(ddx, vh) + dot(ddx, vl)
+    sy[...] = dot(ddy, vh) + dot(ddy, vl)
+    out_ref[...] = mass + apply(0, mass)
+    hand_over(2)
+
+    def add(copies, slot, o):
+        if copies is not None:
+            for copy in copies:
+                copy.wait_recv()
+        out_ref[...] += apply(o + 1, got[slot])
+
+    add(sibling, 2, 2 - 2 * core)
+    add(None, 0, 3 - 2 * odd)
+    add(None, 1, 1 + 2 * odd)
     for o in range(lists):
         coef_copy[o].wait_recv()
-    diagonal = iota((cells, size), 0) == iota((cells, size), 1)
-    for j, w in enumerate((wq, wx, wy)):
-        total = coef[0, j : j + 1, :]
-        for o in range(lists):
-            total = total + coef_got[o, j : j + 1, :]
-        w[...] = w[...] - jnp.where(diagonal, total, 0.0)
-    fold(0)
-    local.wait()
-    mass = own[...]
-    out_ref[...] = mass + apply(0, mass)
-    for o in (2, 0, 3, 1):
-        mass_copy[o].wait_recv()
-        out_ref[...] += apply(o + 1, got[o])
-    for o in range(lists):
-        enc_copy[o].wait_send()
-        mass_copy[o].wait_send()
-        coef_copy[o].wait_send()
+    total = coef[0]
+    for o in range(lists):
+        total = total + coef_got[o]
+    rows[0:8, :] = total
+    cols[...] = rows[...].T
+    out_ref[...] -= (
+        cols[0:cells, 0:1] * own[...] + cols[0:cells, 1:2] * sx[...] + cols[0:cells, 2:3] * sy[...]
+    )
+    add(share, 3, 2 * core)
+    for copy in enc_copy + near + far + sibling + share + coef_copy:
+        copy.wait_send()
 
 
 def local(mesh, tracer_mass, send_ids, send_counts, sources, fractions, moments):
     cells, width = tracer_mass.shape
     lists, slots = send_ids.shape
     size = round_up(cells, LANES)
-    vmem = pl.BlockSpec(memory_space=pltpu.VMEM)
     dma = pltpu.SemaphoreType.DMA
     return pl.pallas_call(
         functools.partial(kernel, mesh.shape["curve"]),
         out_shape=jax.ShapeDtypeStruct((cells, width), F32),
-        in_specs=[
-            pl.BlockSpec(memory_space=pl.ANY),
-            vmem,
-            pl.BlockSpec(memory_space=pltpu.SMEM),
-            vmem,
-            vmem,
-            vmem,
-        ],
-        out_specs=vmem,
+        in_specs=[pl.BlockSpec(memory_space=pl.ANY)] * 6,
+        out_specs=pl.BlockSpec(memory_space=pltpu.VMEM),
         scratch_shapes=[
             pltpu.VMEM((cells, width), F32),
+            pltpu.VMEM(send_ids.shape, jnp.int32),
+            pltpu.SMEM(send_counts.shape, jnp.int32),
+            pltpu.VMEM(sources.shape[::-1], jnp.int32),
+            pltpu.VMEM(fractions.shape[::-1], F32),
+            pltpu.VMEM((2,) + fractions.shape[::-1], F32),
             pltpu.VMEM((lists, cells, width), F32),
             pltpu.VMEM((8, lists * slots), F32),
             pltpu.VMEM((lists, 8, lists * slots), F32),
@@ -236,12 +289,13 @@
             pltpu.VMEM((lists + 1, cells, size), BF16),
             pltpu.VMEM((size, size), BF16),
             pltpu.VMEM((size, size), BF16),
-            dma,
+            pltpu.VMEM((cells, width), F32),
+            pltpu.VMEM((cells, width), F32),
+            dma((6,)),
         ]
-        + [dma((lists,))] * 6,
-        compiler_params=pltpu.CompilerParams(
-            collective_id=0, has_side_effects=True, vmem_limit_bytes=40 * 2**20
-        ),
+        + [dma((lists * PARTS,))] * 2
+        + [dma((lists,))] * 4,
+        compiler_params=pltpu.CompilerParams(collective_id=0, has_side_effects=True),
         name="transport",
     )(tracer_mass, send_ids, send_counts, sources.T, fractions.T, moments.transpose(0, 2, 1))
 

time: 35.3 us -> 27 us (0.76); the launches traced: 34.6 us -> 26.8 us
  Pallas kernels: 30.2 us -> 25.1 us
  local copies, waits for them, and re-layouts: 4.45 us -> 1.69 us
    pallas_call x1, Pallas kernels: 30.2 us -> 25.1 us  [local(): pl.pallas_call(functools.partial(kernel, mesh.shape['curve']), out_shape=...]
    unnamed x13 -> x1, local copies, waits for them, and re-layouts: 4.45 us -> 1.69 us
where the time goes in v2:
time: 27 us; the launch traced here: 26.8 us
  Pallas kernels  25.1 us (93%)
  local copies, waits for them, and re-layouts  1.69 us (6%)
    pallas_call x1, Pallas kernels, local(): pl.pallas_call(functools.partial(kernel, mesh.shape['curve']), out_shape=...  25.1 us
    unnamed x1, local copies, waits for them, and re-layouts  1.69 us

profile of v2, /device:TPU:0, one launch (start us, length us, event | category | flops | bytes accessed | tf_op | source)
XLA Modules:
  0.0 26.8 jit_solution(332460730999759072)
XLA Ops:
  0.0 25.1 %transport.1 = f32[288,200]{1,0:T(8,128)} custom-call(f32[288,200]{1,0:T(8,128)} %mass_hbm.1, s32[4,32]{1,0:T(4,128)} %ids_hbm.1, s32[4]{0:T(128)} %counts_hbm.1, s32[4,288]{1,0:T(4,128)} %bitcast.4, f32[4,288]{1,0:T(4,128)} %bitcast.5, f32[2,4,288]{2,1,0:T(4,128)} %bitcast.3), custom_call_target="tpu_custom_call" | custom-call | tf_op jit(solution)/shard_map/transport/pallas_call | solution.py:266
  25.1 1.7 %copy.8 = f32[288,200]{1,0:T(8,128)} copy(f32[288,200]{1,0:T(8,128)} %transport.1) | data formatting | bytes 460800

commit v3 on v2

--- a/solution.py
+++ b/solution.py
@@ -12,6 +12,7 @@
 LANES = 128
 CHUNK = 32
 PARTS = 3
+UNROLL = 3
 F32 = jnp.float32
 BF16 = jnp.bfloat16
 
@@ -154,6 +155,54 @@
     rows[8 : 8 + pieces, 0:cells] = frac
     rows[16 : 16 + pieces, 0:cells] = frac * mom_ref[0]
     rows[24 : 24 + pieces, 0:cells] = frac * mom_ref[1]
+
+    def build(o):
+        lane_id = (iota((CHUNK, size), 1) + o * block).astype(F32)
+
+        def chunk(start, sums):
+            at_rows = pl.ds(pl.multiple_of(start, CHUNK), CHUNK)
+            q = jnp.zeros((CHUNK, size), F32)
+            x, y = q, q
+            for k in range(pieces):
+                hit = lane_id == cols[at_rows, k : k + 1]
+                q = q + jnp.where(hit, cols[at_rows, 8 + k : 9 + k], 0.0)
+                x = x + jnp.where(hit, cols[at_rows, 16 + k : 17 + k], 0.0)
+                y = y + jnp.where(hit, cols[at_rows, 24 + k : 25 + k], 0.0)
+            wq[at_rows, :] = q
+            wx[at_rows, :] = x
+            wy[at_rows, :] = y
+            return tuple(
+                s + v.reshape(CHUNK // 8, 8, size).sum(0) for s, v in zip(sums, (q, x, y))
+            )
+
+        def step(i, sums):
+            for j in range(UNROLL):
+                sums = chunk((i * UNROLL + j) * CHUNK, sums)
+            return sums
+
+        zero = jnp.zeros((8, size), F32)
+        sums = lax.fori_loop(0, cells // (CHUNK * UNROLL), step, (zero, zero, zero))
+        for j in range(3):
+            coef[o, j : j + 1, :] = jnp.sum(sums[j], axis=0, keepdims=True)
+
+    def fold(o):
+        xh, xl = split(wx[...])
+        yh, yl = split(wy[...])
+        ddx, ddy = dx[...], dy[...]
+        total = wq[...] + dot(xh, ddx) + dot(xl, ddx) + dot(yh, ddy) + dot(yl, ddy)
+        h, l = split(total)
+        high[o] = h
+        low[o] = l
+
+    def apply(o, value):
+        vh, vl = split(value)
+        h, l = high[o, :, 0:cells], low[o, :, 0:cells]
+        return dot(h, vh) + dot(h, vl) + dot(l, vh)
+
+    rows[0:pieces, 0:cells] = jnp.where(element < own_elements, src, -1).astype(F32)
+    cols[...] = rows[...].T
+    coef[0] = jnp.zeros((8, size), F32)
+    build(0)
 
     for o in ORDER:
         enc_copy[o].wait_recv()
@@ -174,65 +223,22 @@
         )
     cols[...] = rows[...].T
 
-    def build(o):
-        lane_id = (iota((CHUNK, size), 1) + o * block).astype(F32)
-
-        def step(i, sums):
-            at_rows = pl.ds(pl.multiple_of(i * CHUNK, CHUNK), CHUNK)
-            q = jnp.zeros((CHUNK, size), F32)
-            x, y = q, q
-            for k in range(pieces):
-                hit = lane_id == cols[at_rows, k : k + 1]
-                q = q + jnp.where(hit, cols[at_rows, 8 + k : 9 + k], 0.0)
-                x = x + jnp.where(hit, cols[at_rows, 16 + k : 17 + k], 0.0)
-                y = y + jnp.where(hit, cols[at_rows, 24 + k : 25 + k], 0.0)
-            wq[at_rows, :] = q
-            wx[at_rows, :] = x
-            wy[at_rows, :] = y
-            return tuple(
-                s + v.reshape(CHUNK // 8, 8, size).sum(0) for s, v in zip(sums, (q, x, y))
-            )
-
-        zero = jnp.zeros((8, size), F32)
-        sums = lax.fori_loop(0, cells // CHUNK, step, (zero, zero, zero))
-        for j in range(3):
-            coef[o, j : j + 1, :] = jnp.sum(sums[j], axis=0, keepdims=True)
-
-    def fold(o):
-        xh, xl = split(wx[...])
-        yh, yl = split(wy[...])
-        ddx, ddy = dx[...], dy[...]
-        total = wq[...] + dot(xh, ddx) + dot(xl, ddx) + dot(yh, ddy) + dot(yl, ddy)
-        h, l = split(total)
-        high[o] = h
-        low[o] = l
-
-    def apply(o, value):
-        vh, vl = split(value)
-        h, l = high[o, :, 0:cells], low[o, :, 0:cells]
-        return dot(h, vh) + dot(h, vl) + dot(l, vh)
-
+    forward(0)
+    fold(0)
+    between = (lambda: forward(1), lambda: forward(2), lambda: hand_over(0), lambda: hand_over(1))
     for o in range(lists):
         coef[o + 1] = jnp.zeros((8, size), F32)
         build(o + 1)
         coef_copy[o].start()
-        if o < PARTS:
-            forward(o)
+        between[o]()
         fold(o + 1)
-    hand_over(0)
-
-    coef[0] = jnp.zeros((8, size), F32)
-    build(0)
-    fold(0)
-    hand_over(1)
     inputs[5].wait()
     mass = own[...]
     vh, vl = split(mass)
     ddx, ddy = dx[0:cells, 0:cells], dy[0:cells, 0:cells]
     sx[...] = dot(ddx, vh) + dot(ddx, vl)
     sy[...] = dot(ddy, vh) + dot(ddy, vl)
-    out_ref[...] = mass + apply(0, mass)
-    hand_over(2)
+    out_ref[...] = apply(0, mass)
 
     def add(copies, slot, o):
         if copies is not None:
@@ -241,6 +247,7 @@
         out_ref[...] += apply(o + 1, got[slot])
 
     add(sibling, 2, 2 - 2 * core)
+    hand_over(2)
     add(None, 0, 3 - 2 * odd)
     add(None, 1, 1 + 2 * odd)
     for o in range(lists):
@@ -263,7 +270,7 @@
     lists, slots = send_ids.shape
     size = round_up(cells, LANES)
     dma = pltpu.SemaphoreType.DMA
-    return pl.pallas_call(
+    change = pl.pallas_call(
         functools.partial(kernel, mesh.shape["curve"]),
         out_shape=jax.ShapeDtypeStruct((cells, width), F32),
         in_specs=[pl.BlockSpec(memory_space=pl.ANY)] * 6,
@@ -298,6 +305,7 @@
         compiler_params=pltpu.CompilerParams(collective_id=0, has_side_effects=True),
         name="transport",
     )(tracer_mass, send_ids, send_counts, sources.T, fractions.T, moments.transpose(0, 2, 1))
+    return tracer_mass + change
 
 
 def solution(mesh):

time: 27 us -> 26 us (0.963)
  other arithmetic: 0 us -> 1.71 us
  local copies, waits for them, and re-layouts: 1.69 us -> 0.01 us
  Pallas kernels: 25.1 us -> 24.2 us
    add x0 -> x1, other arithmetic: none -> 1.71 us  [local(): return tracer_mass + change]
    unnamed x1 -> x2, local copies, waits for them, and re-layouts: 1.69 us -> 0.01 us
    pallas_call x1, Pallas kernels: 25.1 us -> 24.2 us  [local(): pl.pallas_call(functools.partial(kernel, mesh.shape['curve']), out_shape=...]
where the time goes in v3:
time: 26 us; the launch traced here: 25.9 us
  Pallas kernels  24.2 us (93%)
  other arithmetic  1.71 us (7%)
    pallas_call x1, Pallas kernels, local(): pl.pallas_call(functools.partial(kernel, mesh.shape['curve']), out_shape=...  24.2 us
    add x1, other arithmetic, local(): return tracer_mass + change  1.71 us

profile of v3, /device:TPU:0, one launch (start us, length us, event | category | flops | bytes accessed | tf_op | source)
XLA Modules:
  0.0 25.9 jit_solution(5397716677039886049)
XLA Ops:
  0.0 0.0 copy-start
  0.0 24.2 %transport.1 = f32[288,200]{1,0:T(8,128)} custom-call(f32[288,200]{1,0:T(8,128)} %mass_hbm.1, s32[4,32]{1,0:T(4,128)} %ids_hbm.1, s32[4]{0:T(128)} %counts_hbm.1, s32[4,288]{1,0:T(4,128)} %bitcast.4, f32[4,288]{1,0:T(4,128)} %bitcast.5, f32[2,4,288]{2,1,0:T(4,128)} %bitcast.3), custom_call_target="tpu_custom_call" | custom-call | tf_op jit(solution)/shard_map/transport/pallas_call | solution.py:273
  24.2 0.0 copy-done
  24.2 1.7 %add.3 = f32[288,200]{1,0:T(8,128)} add(f32[288,200]{1,0:T(8,128)S(1)} %copy-done, f32[288,200]{1,0:T(8,128)} %transport.1) | non-fusion elementwise | flops 57600 | bytes 691200 | tf_op jit(solution)/shard_map/add | solution.py:308
Async XLA Ops:
  0.0 24.2 %copy-start = (f32[288,200]{1,0:T(8,128)S(1)}, f32[288,200]{1,0:T(8,128)}, u32[]{:S(2)}) copy-start(f32[288,200]{1,0:T(8,128)} %mass_hbm.1) | copy-start | bytes 691204

commit v4 on v3

--- a/solution.py
+++ b/solution.py
@@ -53,7 +53,7 @@
 def kernel(
     count, mass_hbm, ids_hbm, counts_hbm, src_hbm, frac_hbm, mom_hbm, out_ref,
     own, ids_ref, counts_ref, src_ref, frac_ref, mom_ref,
-    got, enc, enc_got, coef, coef_got, rows, cols, wq, wx, wy, high, low, dx, dy, sx, sy,
+    got, enc, enc_got, coef, coef_got, rows, cols, wide_cols, wq, wx, wy, high, low, dx, dy, sx, sy,
     in_sem, mass_send, mass_recv, enc_send, enc_recv, coef_send, coef_recv,
 ):
     cells, width = own.shape
@@ -156,6 +156,18 @@
     rows[16 : 16 + pieces, 0:cells] = frac * mom_ref[0]
     rows[24 : 24 + pieces, 0:cells] = frac * mom_ref[1]
 
+    def fill(kinds):
+        cols[...] = rows[...].T
+        for kind in kinds:
+            for k in range(pieces):
+                lane = 8 * kind + k
+                wide_cols[kind * pieces + k] = jnp.broadcast_to(
+                    cols[0:cells, lane : lane + 1], (cells, LANES)
+                )
+
+    def spread(index, at_rows):
+        return jnp.concatenate([wide_cols[index, at_rows, :]] * (size // LANES), axis=1)
+
     def build(o):
         lane_id = (iota((CHUNK, size), 1) + o * block).astype(F32)
 
@@ -164,10 +176,10 @@
             q = jnp.zeros((CHUNK, size), F32)
             x, y = q, q
             for k in range(pieces):
-                hit = lane_id == cols[at_rows, k : k + 1]
-                q = q + jnp.where(hit, cols[at_rows, 8 + k : 9 + k], 0.0)
-                x = x + jnp.where(hit, cols[at_rows, 16 + k : 17 + k], 0.0)
-                y = y + jnp.where(hit, cols[at_rows, 24 + k : 25 + k], 0.0)
+                hit = lane_id == spread(k, at_rows)
+                q = q + jnp.where(hit, spread(pieces + k, at_rows), 0.0)
+                x = x + jnp.where(hit, spread(2 * pieces + k, at_rows), 0.0)
+                y = y + jnp.where(hit, spread(3 * pieces + k, at_rows), 0.0)
             wq[at_rows, :] = q
             wx[at_rows, :] = x
             wy[at_rows, :] = y
@@ -200,7 +212,7 @@
         return dot(h, vh) + dot(h, vl) + dot(l, vh)
 
     rows[0:pieces, 0:cells] = jnp.where(element < own_elements, src, -1).astype(F32)
-    cols[...] = rows[...].T
+    fill(range(4))
     coef[0] = jnp.zeros((8, size), F32)
     build(0)
 
@@ -221,7 +233,7 @@
         rows[k : k + 1, 0:cells] = jnp.where(
             e < own_elements, src[k : k + 1, :].astype(F32), jnp.where(found > 0.5, moved, -1.0)
         )
-    cols[...] = rows[...].T
+    fill(range(1))
 
     forward(0)
     fold(0)
@@ -289,6 +301,7 @@
             pltpu.VMEM((lists, 8, size), F32),
             pltpu.VMEM((LANES, size), F32),
             pltpu.VMEM((size, LANES), F32),
+            pltpu.VMEM((4 * sources.shape[1], cells, LANES), F32),
             pltpu.VMEM((cells, size), F32),
             pltpu.VMEM((cells, size), F32),
             pltpu.VMEM((cells, size), F32),

time: 26 us -> 25.3 us (0.973)
  Pallas kernels: 24.2 us -> 23.4 us
    pallas_call x1, Pallas kernels: 24.2 us -> 23.4 us  [local(): pl.pallas_call(functools.partial(kernel, mesh.shape['curve']), out_shape=...]
where the time goes in v4:
time: 25.3 us; the launch traced here: 25.2 us
  Pallas kernels  23.4 us (92%)
  other arithmetic  1.71 us (7%)
    pallas_call x1, Pallas kernels, local(): pl.pallas_call(functools.partial(kernel, mesh.shape['curve']), out_shape=...  23.4 us
    add x1, other arithmetic, local(): return tracer_mass + change  1.71 us

profile of v4, /device:TPU:0, one launch (start us, length us, event | category | flops | bytes accessed | tf_op | source)
XLA Modules:
  0.0 25.2 jit_solution(5011498243759786179)
XLA Ops:
  0.0 0.0 copy-start
  0.0 23.4 %transport.1 = f32[288,200]{1,0:T(8,128)} custom-call(f32[288,200]{1,0:T(8,128)} %mass_hbm.1, s32[4,32]{1,0:T(4,128)} %ids_hbm.1, s32[4]{0:T(128)} %counts_hbm.1, s32[4,288]{1,0:T(4,128)} %bitcast.4, f32[4,288]{1,0:T(4,128)} %bitcast.5, f32[2,4,288]{2,1,0:T(4,128)} %bitcast.3), custom_call_target="tpu_custom_call" | custom-call | tf_op jit(solution)/shard_map/transport/pallas_call | solution.py:285
  23.5 0.0 copy-done
  23.5 1.7 %add.3 = f32[288,200]{1,0:T(8,128)} add(f32[288,200]{1,0:T(8,128)S(1)} %copy-done, f32[288,200]{1,0:T(8,128)} %transport.1) | non-fusion elementwise | flops 57600 | bytes 691200 | tf_op jit(solution)/shard_map/add | solution.py:321
Async XLA Ops:
  0.0 23.5 %copy-start = (f32[288,200]{1,0:T(8,128)S(1)}, f32[288,200]{1,0:T(8,128)}, u32[]{:S(2)}) copy-start(f32[288,200]{1,0:T(8,128)} %mass_hbm.1) | copy-start | bytes 691204

commit v5 on v4

--- a/solution.py
+++ b/solution.py
@@ -201,7 +201,8 @@
         xh, xl = split(wx[...])
         yh, yl = split(wy[...])
         ddx, ddy = dx[...], dy[...]
-        total = wq[...] + dot(xh, ddx) + dot(xl, ddx) + dot(yh, ddy) + dot(yl, ddy)
+        parts = jnp.concatenate([xh, xl, yh, yl], axis=1)
+        total = wq[...] + dot(parts, jnp.concatenate([ddx, ddx, ddy, ddy], axis=0))
         h, l = split(total)
         high[o] = h
         low[o] = l

time: 25.3 us -> 25.1 us (level)
  no operation moved by 1% of the time
where the time goes in v5:
time: 25.1 us; the launch traced here: 25 us
  Pallas kernels  23.2 us (92%)
  other arithmetic  1.71 us (7%)
    pallas_call x1, Pallas kernels, local(): pl.pallas_call(functools.partial(kernel, mesh.shape['curve']), out_shape=...  23.2 us
    add x1, other arithmetic, local(): return tracer_mass + change  1.71 us

profile of v5, /device:TPU:0, one launch (start us, length us, event | category | flops | bytes accessed | tf_op | source)
XLA Modules:
  0.0 25.0 jit_solution(10695856139491296530)
XLA Ops:
  0.0 0.0 copy-start
  0.0 23.2 %transport.1 = f32[288,200]{1,0:T(8,128)} custom-call(f32[288,200]{1,0:T(8,128)} %mass_hbm.1, s32[4,32]{1,0:T(4,128)} %ids_hbm.1, s32[4]{0:T(128)} %counts_hbm.1, s32[4,288]{1,0:T(4,128)} %bitcast.4, f32[4,288]{1,0:T(4,128)} %bitcast.5, f32[2,4,288]{2,1,0:T(4,128)} %bitcast.3), custom_call_target="tpu_custom_call" | custom-call | tf_op jit(solution)/shard_map/transport/pallas_call | solution.py:286
  23.3 0.0 copy-done
  23.3 1.7 %add.3 = f32[288,200]{1,0:T(8,128)} add(f32[288,200]{1,0:T(8,128)S(1)} %copy-done, f32[288,200]{1,0:T(8,128)} %transport.1) | non-fusion elementwise | flops 57600 | bytes 691200 | tf_op jit(solution)/shard_map/add | solution.py:322
Async XLA Ops:
  0.0 23.3 %copy-start = (f32[288,200]{1,0:T(8,128)S(1)}, f32[288,200]{1,0:T(8,128)}, u32[]{:S(2)}) copy-start(f32[288,200]{1,0:T(8,128)} %mass_hbm.1) | copy-start | bytes 691204
